TPU v7x, 32 devices: a whole 2x2x4 slice. The times are simulated.
32 devices in a mesh: slab: 2 (over x), ex: 16 (over z, y, core).
Axes of the slice: x: 2, y: 2, z: 4, core: 2. Of those that a mesh axis runs over, the one named last changes fastest.
Arguments:
- train_grads: bfloat16 [16384, 12, 256], P(('slab', 'ex')), parts along dimension 0, may hold values from -2200 to 2200
- queries: bfloat16 [384, 12, 256], P('ex'), may hold values from -6 to 6
- basis: bfloat16 [12, 256, 256], replicated, may hold values from -0.5 to 2.5
Outputs:
- scores: float32 [384, 16384], P(None, ('slab', 'ex')), parts along dimension 1
There are 2 independent parts, one for each index of `slab`. A program takes and returns all parts, laid end to end along the dimension named above; an argument that names none is the same for every part. Nothing has to cross between parts.
All inputs are finite; a program needn't handle non-finite values.
Results may differ from a plain program's by a relative error of at most 0.0042.
Values may be sent and summed in bfloat16 or wider, within the bound.
A program may use at most 128 MiB of HBM per device.

v0:
```python
import jax
import jax.numpy as jnp
from jax import lax
from jax.sharding import PartitionSpec as P


def precondition(q_block, damped, basis):
    qrot = jnp.einsum("qlr,lrs->qls", q_block, basis, preferred_element_type=jnp.float32)
    scaled = (qrot / damped).astype(jnp.bfloat16)
    return jnp.einsum("qls,lrs->qlr", scaled, basis, preferred_element_type=jnp.float32).astype(
        jnp.bfloat16
    )


def local(train_grads, queries, basis):
    ex_rows, layers, feature = train_grads.shape
    rotated = jnp.einsum("ilr,lrs->ils", train_grads, basis, preferred_element_type=jnp.float32)
    local_sq = jnp.sum(rotated * rotated, axis=0)
    total_sq = lax.psum(local_sq, "ex")
    eigvals = total_sq / (ex_rows * lax.axis_size("ex"))
    damped = eigvals + 0.1 * jnp.mean(eigvals, axis=1, keepdims=True)
    flat_grads = train_grads.reshape(ex_rows, layers * feature)
    precond = precondition(queries, damped, basis)
    q_block = lax.all_gather(precond, "ex", axis=0, tiled=True)
    flat_q = q_block.reshape(q_block.shape[0], layers * feature)
    return lax.dot_general(
        flat_q, flat_grads, (((1,), (1,)), ((), ())), preferred_element_type=jnp.float32
    )


def solution(mesh):
    placed = (P(("slab", "ex"), None, None), P("ex", None, None), P())
    return jax.shard_map(
        local, mesh=mesh, in_specs=placed, out_specs=P(None, ("slab", "ex")), check_vma=False
    )
```

profile of v0, /device:TPU:0, one launch (start us, length us, event | category | flops | bytes accessed | tf_op | source)
XLA Modules:
  0.0 128.8 jit_solution(2706144519936346779)
XLA Ops:
  6.5 0.0 copy-start
  6.5 0.0 copy-start.1
  6.5 0.0 all-gather.2.cloned.1.call-start
  6.5 1.9 %copy-done = bf16[512,12,256]{2,0,1:T(8,128)(2,1)S(1)} copy-done((bf16[512,12,256]{2,0,1:T(8,128)(2,1)S(1)}, bf16[512,12,256]{2,0,1:T(8,128)(2,1)}, u32[]{:S(2)}) %copy-start) | copy-done | bytes 3145752
  8.4 2.8 %multiply_reduce_fusion = f32[12,256]{1,0:T(8,128)S(1)} fusion(bf16[12,256,256]{2,1,0:T(8,128)(2,1)} %param.5, bf16[512,12,256]{2,0,1:T(8,128)(2,1)S(1)} %copy-done), kind=kOutput, calls=%fused_computation | convolution fusion | flops 808449024 | bytes 4730880 | tf_op jit(solution)/shard_map/ilr,lrs->ils/dot_general | solution.py:17
  11.2 63.0 %psum.7 = f32[12,256]{1,0:T(8,128)S(1)} all-reduce(f32[12,256]{1,0:T(8,128)S(1)} %multiply_reduce_fusion), channel_id=1, replica_groups=mesh['slab'=2,'ex'=16] {'ex'}, use_global_device_ids=true, to_apply=%region_1.0 | all-reduce | flops 3072 | bytes 24576 | tf_op jit(solution)/shard_map/psum | solution.py:19
  74.2 0.1 multiply_reduce_fusion.1
  74.3 0.1 multiply_add_fusion
  74.4 0.0 copy-done.1
  74.4 3.3 %fusion.1 = bf16[24,12,256]{2,0,1:T(8,128)(2,1)} fusion(bf16[12,256,256]{2,1,0:T(8,128)(2,1)} %param.5, bf16[24,12,256]{2,0,1:T(8,128)(2,1)S(1)} %copy-done.1, f32[12,256]{1,0:T(8,128)S(1)} %multiply_add_fusion), kind=kOutput, calls=%fused_computation.5 | convolution fusion | flops 75718656 | bytes 1880064 | tf_op jit(solution)/shard_map/qls,lrs->qlr/dot_general | solution.py:10
  77.6 0.0 all-gather.2.cloned.1.call-update
  77.7 40.3 %all-gather.2.cloned.1.call-done = bf16[384,12,256]{2,0,1:T(8,128)(2,1)} async-done(((bf16[24,12,256]{2,0,1:T(8,128)(2,1)}), bf16[384,12,256]{2,0,1:T(8,128)(2,1)}) %all-gather.2.cloned.1.call-update) | async-done | bytes 2359312 | tf_op jit(solution)/shard_map/all_gather | solution.py:24
  118.0 4.0 %convolution_bitcast_fusion = f32[384,512]{1,0:T(8,128)} fusion(bf16[384,12,256]{2,0,1:T(8,128)(2,1)} %all-gather.2.cloned.1.call-done, bf16[512,12,256]{2,0,1:T(8,128)(2,1)S(1)} %copy-done), kind=kOutput, calls=%fused_computation.1 | convolution fusion | flops 1207959552 | bytes 6291456 | tf_op jit(solution)/shard_map/dot_general | solution.py:26
  (1 shorter events, 0.0 us)
Async XLA Ops:
  6.5 1.9 %copy-start = (bf16[512,12,256]{2,0,1:T(8,128)(2,1)S(1)}, bf16[512,12,256]{2,0,1:T(8,128)(2,1)}, u32[]{:S(2)}) copy-start(bf16[512,12,256]{2,0,1:T(8,128)(2,1)} %param.3) | copy-start | bytes 9437188
  6.5 67.8 %copy-start.1 = (bf16[24,12,256]{2,0,1:T(8,128)(2,1)S(1)}, bf16[24,12,256]{2,0,1:T(8,128)(2,1)}, u32[]{:S(2)}) copy-start(bf16[24,12,256]{2,0,1:T(8,128)(2,1)} %param.4) | copy-start | bytes 442372
  6.5 111.4 %all-gather.2.cloned.1.call-start = ((), (), s32[]{:S(2)}) async-start(), calls=%async_computation | async-start | bytes 2506752 | tf_op jit(solution)/shard_map/all_gather | solution.py:24
Sparse Core Ops, SparseCore 0:
  77.8 40.1 all-gather.1
where the time goes:
time: 129 us
  blocking collectives  63 us (49%)
  waiting for transfers between devices  40.3 us (31%)
  between operations  13.4 us (10%)
  matrix products  10 us (8%)
  local copies, waits for them, and re-layouts  1.89 us (1%)
    psum x1, blocking collectives, local(): total_sq = lax.psum(local_sq, 'ex')  63 us
    all_gather x1, waiting for transfers between devices, local(): q_block = lax.all_gather(precond, 'ex', axis=0, tiled=True)  40.3 us
    dot_general x1, matrix products, local(): lax.dot_general(flat_q, flat_grads, (((1,), (1,)), ((), ())), preferred_e...  3.96 us
    dot_general x1, matrix products, precondition(): jnp.einsum('qls,lrs->qlr', scaled, basis, preferred_element_type=jnp.floa...  3.28 us
    dot_general x1, matrix products, local(): jnp.einsum('ilr,lrs->ils', train_grads, basis, preferred_element_type=jnp...  2.77 us
  transfers between devices with their start and end apart: 1, of which 1 were waited for; matrix products, arithmetic and copies ran while one was open for 0% of the time, Pallas kernels for 0%

commit v1 on v0

v1 whole, which is shorter than its diff:
```python
import functools
import math

import jax
import jax.numpy as jnp
from jax import lax
from jax.experimental import pallas as pl
from jax.experimental.pallas import tpu as pltpu
from jax.sharding import PartitionSpec as P

MESH = pl.DeviceIdType.MESH
NT = (((1,), (1,)), ((), ()))


def loop(count, body):
    if count <= 4:
        for i in range(count):
            body(i)
    else:
        pl.loop(0, count)(body)


def kernel(
    A, B, t_hbm, q_hbm, b_hbm, out_hbm,
    tv, bv, rot, g, qall, sq, sq1, sq2, ov,
    t_sem, b_sem, own_sem, out_sem, recv, z_send, y_send, x_send, c_send, s1_send, s2_send, s1_recv, s2_recv,
):
    layers, rows, feature = tv.shape
    half = A * B
    total = 2 * half
    blk = ov.shape[1]
    part = layers // 4
    s = lax.axis_index("slab")
    e = lax.axis_index("ex")
    c = lax.rem(e, 2)
    ab = lax.div(e, 2)
    a = lax.div(ab, B)
    b = lax.rem(ab, B)

    def ex_of(a_, b_, c_):
        return (a_ * B + b_) * 2 + c_

    def at(a_, b_, c_, p):
        return (c_ * half + a_ * B + b_) * 4 + p

    def t_copy(l):
        return pltpu.make_async_copy(t_hbm.at[l], tv.at[l], t_sem.at[l])

    def b_copy(l):
        return pltpu.make_async_copy(b_hbm.at[l], bv.at[l], b_sem.at[l])

    for l in range(layers):
        t_copy(l).start()
        b_copy(l).start()
    own = pltpu.make_async_copy(q_hbm, qall.at[pl.ds(at(a, b, c, 0), 4)], own_sem)
    own.start()

    barrier = pltpu.get_barrier_semaphore()

    def greet(device):
        pl.semaphore_signal(barrier, inc=1, device_id=device, device_id_type=MESH)

    loop(A - 1, lambda i: greet((s, ex_of(lax.rem(a + 1 + i, A), b, c))))
    loop(B - 1, lambda i: greet((s, ex_of(a, lax.rem(b + 1 + i, B), c))))
    loop(B, lambda i: greet((s, ex_of(a, lax.rem(b + i, B), 1 - c))))
    greet((1 - s, e))
    pl.semaphore_wait(barrier, A - 1 + 2 * B - 1 + 1)

    def send(src, idx, send_sem, device):
        pltpu.make_async_remote_copy(
            src_ref=src, dst_ref=qall.at[idx], send_sem=send_sem, recv_sem=recv.at[idx],
            device_id=device, device_id_type=MESH,
        ).start()

    def arrived(idx):
        pltpu.make_async_copy(qall.at[idx], qall.at[idx], recv.at[idx]).wait()

    def to_y(src, idx):
        loop(B - 1, lambda i: send(src, idx, y_send, (s, ex_of(a, lax.rem(b + 1 + i, B), c))))

    def to_x(src, idx):
        send(src, idx, x_send, (1 - s, e))

    def to_core(src, idx):
        send(src, idx, c_send, (s, ex_of(a, b, 1 - c)))

    mine = 2 * s
    theirs = 2 - 2 * s

    def send_line(i):
        peer = (s, ex_of(lax.rem(a + 1 + i, A), b, c))
        for t in range(2):
            send(q_hbm.at[mine + t], at(a, b, c, mine + t), z_send, peer)

    loop(A - 1, send_line)
    for p in (mine + 1, mine, theirs):
        to_y(q_hbm.at[p], at(a, b, c, p))
    for p in range(4):
        to_core(q_hbm.at[p], at(a, b, c, p))

    def rotate(l):
        t_copy(l).wait()
        b_copy(l).wait()
        r = jnp.dot(tv[l], bv[l], preferred_element_type=jnp.float32)
        rot[l] = r
        sq[pl.ds(l, 1), :] = jnp.sum(r * r, axis=0, keepdims=True)

    def near(i):
        b_ = lax.rem(b + 1 + i, B)
        idx = at(a, b_, c, mine + 1)
        arrived(idx)
        to_x(qall.at[idx], idx)
        to_core(qall.at[idx], idx)
        for p in (mine, theirs):
            idx = at(a, b_, c, p)
            arrived(idx)
            to_core(qall.at[idx], idx)

    def line(i):
        a_ = lax.rem(a + 1 + i, A)
        for t in (1, 0):
            idx = at(a_, b, c, mine + t)
            arrived(idx)
            to_y(qall.at[idx], idx)
            to_x(qall.at[idx], idx)
            to_core(qall.at[idx], idx)

    def across(i):
        a_ = lax.rem(a + 1 + i, A)
        idx = at(a_, b, c, theirs)
        arrived(idx)
        to_y(qall.at[idx], idx)
        to_core(qall.at[idx], idx)
        idx = at(a_, b, c, theirs + 1)
        arrived(idx)
        to_core(qall.at[idx], idx)

    def far_y(i):
        a_ = lax.rem(a + 1 + i, A)

        def one(j):
            b_ = lax.rem(b + 1 + j, B)
            idx = at(a_, b_, c, mine + 1)
            arrived(idx)
            to_x(qall.at[idx], idx)
            to_core(qall.at[idx], idx)
            idx = at(a_, b_, c, mine)
            arrived(idx)
            to_core(qall.at[idx], idx)

        loop(B - 1, one)

    def far_yy(i):
        a_ = lax.rem(a + 1 + i, A)

        def one(j):
            idx = at(a_, lax.rem(b + 1 + j, B), c, theirs)
            arrived(idx)
            to_core(qall.at[idx], idx)

        loop(B - 1, one)

    def far_x(i):
        a_ = lax.rem(a + i, A)

        def one(j):
            idx = at(a_, lax.rem(b + 1 + j, B), c, theirs + 1)
            arrived(idx)
            to_core(qall.at[idx], idx)

        loop(B - 1, one)

    def sq1_copy(b_, c_):
        slot = b * 2 + c
        return pltpu.make_async_remote_copy(
            src_ref=sq, dst_ref=sq1.at[slot], send_sem=s1_send, recv_sem=s1_recv.at[slot],
            device_id=(s, ex_of(a, b_, c_)), device_id_type=MESH,
        )

    def sq2_copy(a_):
        return pltpu.make_async_remote_copy(
            src_ref=sq2.at[a], dst_ref=sq2.at[a], send_sem=s2_send, recv_sem=s2_recv.at[a],
            device_id=(s, ex_of(a_, b, c)), device_id_type=MESH,
        )

    for l in range(layers):
        rotate(l)
        if l == layers // 2:
            loop(B - 1, near)
    sq1[b * 2 + c] = sq[...]
    loop(B - 1, lambda i: sq1_copy(lax.rem(b + 1 + i, B), c).start())
    loop(B, lambda i: sq1_copy(lax.rem(b + i, B), 1 - c).start())

    line(0)

    def sq1_arrived(b_, c_):
        slot = b_ * 2 + c_
        pltpu.make_async_copy(sq1.at[slot], sq1.at[slot], s1_recv.at[slot]).wait()

    loop(B - 1, lambda i: sq1_arrived(lax.rem(b + 1 + i, B), c))
    loop(B, lambda i: sq1_arrived(lax.rem(b + i, B), 1 - c))
    acc = sq1[0]
    for i in range(1, 2 * B):
        acc = acc + sq1[i]
    sq2[a] = acc
    loop(A - 1, lambda i: sq2_copy(lax.rem(a + 1 + i, A)).start())

    loop(A - 2, lambda i: line(i + 1))
    loop(A - 1, across)

    def sq2_arrived(i):
        slot = lax.rem(a + 1 + i, A)
        pltpu.make_async_copy(sq2.at[slot], sq2.at[slot], s2_recv.at[slot]).wait()

    loop(A - 1, sq2_arrived)
    acc = sq2[0]
    for i in range(1, A):
        acc = acc + sq2[i]
    eig = acc / (rows * total)
    damped = eig + 0.1 * jnp.mean(eig, axis=1, keepdims=True)
    inv = 1.0 / damped

    def project(l):
        scaled = (rot[l] * inv[l : l + 1, :]).astype(jnp.bfloat16)
        g[:, l * feature : (l + 1) * feature] = lax.dot_general(
            scaled, bv[l], NT, preferred_element_type=jnp.float32
        ).astype(jnp.bfloat16)

    for l in range(0, layers // 3):
        project(l)
    loop(A - 1, far_y)
    for l in range(layers // 3, 2 * layers // 3):
        project(l)
    loop(A - 1, far_yy)
    for l in range(2 * layers // 3, layers):
        project(l)
    loop(A, far_x)
    own.wait()

    group = math.gcd(half, 8)
    chunks = half // group

    def score(first):
        cols = []
        for p in range(4):
            for j in range(part):
                cols.append(
                    jnp.concatenate(
                        [qall[(first + i) * 4 + p, j].astype(jnp.float32) for i in range(group)], axis=0
                    ).astype(jnp.bfloat16)
                )
        q = jnp.concatenate(cols, axis=1)
        r = lax.dot_general(q, g[...], NT, preferred_element_type=jnp.float32)
        return r.reshape(group, blk, rows)

    def out_copy(c_, k):
        return pltpu.make_async_copy(
            ov.at[pl.ds(c_ * half + k * group, group)],
            out_hbm.at[pl.ds(k * group, group), c_],
            out_sem.at[c_, k],
        )

    def do_chunk(c_, k):
        first = c_ * half + k * group
        ov[pl.ds(first, group)] = score(first)
        out_copy(c_, k).start()

    loop(chunks, lambda k: do_chunk(c, k))

    def mate(i):
        for p in range(4):
            arrived(((1 - c) * half + i) * 4 + p)

    pl.loop(0, half)(mate)
    loop(chunks, lambda k: do_chunk(1 - c, k))

    def drain(count, sem):
        pltpu.make_async_copy(qall.at[pl.ds(0, count)], qall.at[pl.ds(0, count)], sem).wait()

    drain(2 * (A - 1), z_send)
    drain(3 * A * (B - 1), y_send)
    drain(2 * (A - 1) + A * (B - 1), x_send)
    drain(4 * half, c_send)
    pltpu.make_async_copy(sq1.at[pl.ds(0, 2 * B - 1)], sq1.at[pl.ds(0, 2 * B - 1)], s1_send).wait()
    pltpu.make_async_copy(sq2.at[pl.ds(0, A - 1)], sq2.at[pl.ds(0, A - 1)], s2_send).wait()
    for c_ in range(2):
        loop(chunks, lambda k: out_copy(c_, k).wait())


def local(n, train_grads, queries, basis):
    rows, layers, feature = train_grads.shape
    blk = queries.shape[0]
    half = n // 2
    A = 2 ** ((half.bit_length()) // 2)
    B = half // A
    t = train_grads.transpose(1, 0, 2)
    q = queries.transpose(1, 0, 2).reshape(4, layers // 4, blk, feature)
    group = math.gcd(half, 8)
    dma = pltpu.SemaphoreType.DMA
    anyspec = pl.BlockSpec(memory_space=pl.ANY)
    out = pl.pallas_call(
        functools.partial(kernel, A, B),
        out_shape=jax.ShapeDtypeStruct((half, 2, blk, rows), jnp.float32),
        in_specs=[anyspec] * 3,
        out_specs=anyspec,
        scratch_shapes=[
            pltpu.VMEM((layers, rows, feature), jnp.bfloat16),
            pltpu.VMEM((layers, feature, feature), jnp.bfloat16),
            pltpu.VMEM((layers, rows, feature), jnp.float32),
            pltpu.VMEM((rows, layers * feature), jnp.bfloat16),
            pltpu.VMEM((n * 4, layers // 4, blk, feature), jnp.bfloat16),
            pltpu.VMEM((layers, feature), jnp.float32),
            pltpu.VMEM((2 * B, layers, feature), jnp.float32),
            pltpu.VMEM((A, layers, feature), jnp.float32),
            pltpu.VMEM((n, blk, rows), jnp.float32),
            dma((layers,)),
            dma((layers,)),
            dma,
            dma((2, half // group)),
            dma((n * 4,)),
            dma, dma, dma, dma, dma, dma,
            dma((2 * B,)),
            dma((A,)),
        ],
        compiler_params=pltpu.CompilerParams(
            collective_id=0, has_side_effects=True, vmem_limit_bytes=56 * 1024 * 1024
        ),
        cost_estimate=pl.CostEstimate(
            flops=4 * layers * rows * feature * feature + 2 * n * blk * rows * layers * feature,
            bytes_accessed=2 * layers * feature * (rows + feature + blk) + 4 * n * blk * rows,
            transcendentals=0,
        ),
    )(t, q, basis)
    return out.reshape(n * blk, rows)


def solution(mesh):
    placed = (P(("slab", "ex"), None, None), P("ex", None, None), P())
    return jax.shard_map(
        functools.partial(local, mesh.shape["ex"]), mesh=mesh, in_specs=placed,
        out_specs=P(None, ("slab", "ex")), check_vma=False,
    )
```

time: 129 us -> 29.5 us (0.23)
  blocking collectives: 63 us -> 0 us
  waiting for transfers between devices: 40.3 us -> 0 us
  Pallas kernels: 0 us -> 27.3 us
  between operations: 13.4 us -> 0.01 us
  matrix products: 10 us -> 0 us
    psum x1 -> x0, blocking collectives: 63 us -> none  [local(): total_sq = lax.psum(local_sq, 'ex')]
    all_gather x1 -> x0, waiting for transfers between devices: 40.3 us -> none  [local(): q_block = lax.all_gather(precond, 'ex', axis=0, tiled=True)]
    pallas_call x0 -> x1, Pallas kernels: none -> 27.3 us  [local(): pl.pallas_call(functools.partial(kernel, A, B), out_shape=jax.ShapeDtypeS...]
    dot_general x3 -> x0, matrix products: 10 us -> none  [the longest x1 3.96 us: local(): lax.dot_general(flat_q, flat_grads, (((1,), (1,)), ((), ())), preferred_e...]
  transfers between devices with their start and end apart: 1 -> 0, of which waited for: 1 -> 0; matrix products, arithmetic and copies ran while one was open for 0% -> 0% of each run, Pallas kernels for 0% -> 0%
where the time goes in v1:
time: 29.5 us; the launch traced here: 29.3 us
  Pallas kernels  27.3 us (93%)
  local copies, waits for them, and re-layouts  2.06 us (7%)
    pallas_call x1, Pallas kernels, local(): pl.pallas_call(functools.partial(kernel, A, B), out_shape=jax.ShapeDtypeS...  27.3 us
    unnamed x1, local copies, waits for them, and re-layouts  2.06 us

profile of v1, /device:TPU:0, one launch (start us, length us, event | category | flops | bytes accessed | tf_op | source)
XLA Modules:
  0.0 29.3 jit_solution(3852775408144678194)
XLA Ops:
  0.0 27.3 %shard_map.37 = f32[8,2,24,512]{3,2,1,0:T(8,128)} custom-call(bf16[12,512,256]{2,1,0:T(8,128)(2,1)} %bitcast.6, bf16[4,3,24,256]{3,2,1,0:T(8,128)(2,1)} %bitcast.7, bf16[12,256,256]{2,1,0:T(8,128)(2,1)} %b_hbm.1), custom_call_target="tpu_custom_call" | custom-call | flops 2818572288 | bytes 5652480 | tf_op jit(solution)/shard_map/pallas_call | solution.py:301
  27.3 2.1 %copy.5 = f32[384,512]{1,0:T(8,128)} copy(f32[384,512]{1,0:T(8,128)} %bitcast.5) | data formatting | bytes 1572864

commit v2 on v1

v2 whole, which is shorter than its diff:
```python
import functools
import math

import jax
import jax.numpy as jnp
from jax import lax
from jax.experimental import pallas as pl
from jax.experimental.pallas import tpu as pltpu
from jax.sharding import PartitionSpec as P

VMEM_BYTES = 53 * 1024 * 1024
MESH = pl.DeviceIdType.MESH
NT = (((1,), (1,)), ((), ()))


def loop(count, body):
    if count <= 4:
        for i in range(count):
            body(i)
    else:
        pl.loop(0, count)(body)


def kernel(
    A, B, t_hbm, q_hbm, b_hbm, out_ref,
    tv, bv, rot, g, qall, sq, sq1, sq2,
    t_sem, b_sem, own_sem, recv, z_send, y_send, x_send, c_send, s1_send, s2_send, s1_recv, s2_recv,
):
    layers, rows, feature = tv.shape
    half = A * B
    total = 2 * half
    blk = qall.shape[2]
    part = layers // 4
    s = lax.axis_index("slab")
    e = lax.axis_index("ex")
    c = lax.rem(e, 2)
    ab = lax.div(e, 2)
    a = lax.div(ab, B)
    b = lax.rem(ab, B)

    def ex_of(a_, b_, c_):
        return (a_ * B + b_) * 2 + c_

    def at(a_, b_, c_, p):
        return (c_ * half + a_ * B + b_) * 4 + p

    def t_copy(l):
        return pltpu.make_async_copy(t_hbm.at[l], tv.at[l], t_sem.at[l])

    def b_copy(l):
        return pltpu.make_async_copy(b_hbm.at[l], bv.at[l], b_sem.at[l])

    for l in range(layers):
        t_copy(l).start()
        b_copy(l).start()
    own = pltpu.make_async_copy(q_hbm, qall.at[pl.ds(at(a, b, c, 0), 4)], own_sem)
    own.start()

    barrier = pltpu.get_barrier_semaphore()

    def greet(device):
        pl.semaphore_signal(barrier, inc=1, device_id=device, device_id_type=MESH)

    loop(A - 1, lambda i: greet((s, ex_of(lax.rem(a + 1 + i, A), b, c))))
    loop(B - 1, lambda i: greet((s, ex_of(a, lax.rem(b + 1 + i, B), c))))
    loop(B, lambda i: greet((s, ex_of(a, lax.rem(b + i, B), 1 - c))))
    greet((1 - s, e))
    def rotate(l):
        t_copy(l).wait()
        b_copy(l).wait()
        r = jnp.dot(tv[l], bv[l], preferred_element_type=jnp.float32)
        rot[l] = r
        sq[pl.ds(l, 1), :] = jnp.sum(r * r, axis=0, keepdims=True)

    for l in range(layers // 2):
        rotate(l)
    pl.semaphore_wait(barrier, A - 1 + 2 * B - 1 + 1)

    def send(src, idx, send_sem, device):
        pltpu.make_async_remote_copy(
            src_ref=src, dst_ref=qall.at[idx], send_sem=send_sem, recv_sem=recv.at[idx],
            device_id=device, device_id_type=MESH,
        ).start()

    def arrived(idx):
        pltpu.make_async_copy(qall.at[idx], qall.at[idx], recv.at[idx]).wait()

    def to_y(src, idx):
        loop(B - 1, lambda i: send(src, idx, y_send, (s, ex_of(a, lax.rem(b + 1 + i, B), c))))

    def to_x(src, idx):
        send(src, idx, x_send, (1 - s, e))

    def to_core(src, idx):
        send(src, idx, c_send, (s, ex_of(a, b, 1 - c)))

    mine = 2 * s
    theirs = 2 - 2 * s

    def others(k, body):
        for ahead, there in ((1, a >= k), (-1, a < A - k)):

            @pl.when(there)
            def _():
                body(a - ahead * k)

    def send_line(a_):
        for t in (1, 0):
            send(q_hbm.at[mine + t], at(a, b, c, mine + t), z_send, (s, ex_of(a_, b, c)))

    others(1, send_line)
    for p in (mine + 1, mine, theirs):
        to_y(q_hbm.at[p], at(a, b, c, p))
    for k in range(2, A):
        others(k, send_line)
    for p in range(4):
        to_core(q_hbm.at[p], at(a, b, c, p))

    def near(i):
        b_ = lax.rem(b + 1 + i, B)
        idx = at(a, b_, c, mine + 1)
        arrived(idx)
        to_x(qall.at[idx], idx)
        to_core(qall.at[idx], idx)
        for p in (mine, theirs):
            idx = at(a, b_, c, p)
            arrived(idx)
            to_core(qall.at[idx], idx)

    def line(k):
        def one(a_):
            for t in (1, 0):
                idx = at(a_, b, c, mine + t)
                arrived(idx)

                if t == 1:
                    to_y(qall.at[idx], idx)
                    to_x(qall.at[idx], idx)
                else:
                    to_x(qall.at[idx], idx)
                    to_y(qall.at[idx], idx)
                to_core(qall.at[idx], idx)

        others(k, one)

    def across(k):
        def one(a_):
            idx = at(a_, b, c, theirs)
            arrived(idx)
            to_y(qall.at[idx], idx)
            to_core(qall.at[idx], idx)

        others(k, one)

    def columns(body):
        loop(B - 1, lambda j: body(lax.rem(b + 1 + j, B)))

    def far_y(k):
        def one(a_):
            def col(b_):
                idx = at(a_, b_, c, mine + 1)
                arrived(idx)
                to_x(qall.at[idx], idx)
                to_core(qall.at[idx], idx)

            columns(col)

        others(k, one)

    def last(idx):
        arrived(idx)
        to_core(qall.at[idx], idx)

    def rest(k):
        def one(a_):
            last(at(a_, b, c, theirs + 1))
            columns(lambda b_: last(at(a_, b_, c, mine)))

        others(k, one)

    def rest_far(k):
        def one(a_):
            columns(lambda b_: last(at(a_, b_, c, theirs)))
            columns(lambda b_: last(at(a_, b_, c, theirs + 1)))

        others(k, one)

    def sq1_copy(b_, c_):
        slot = b * 2 + c
        return pltpu.make_async_remote_copy(
            src_ref=sq, dst_ref=sq1.at[slot], send_sem=s1_send, recv_sem=s1_recv.at[slot],
            device_id=(s, ex_of(a, b_, c_)), device_id_type=MESH,
        )

    def sq2_copy(a_):
        return pltpu.make_async_remote_copy(
            src_ref=sq2.at[a], dst_ref=sq2.at[a], send_sem=s2_send, recv_sem=s2_recv.at[a],
            device_id=(s, ex_of(a_, b, c)), device_id_type=MESH,
        )

    for l in range(layers // 2, layers):
        rotate(l)
    sq1[b * 2 + c] = sq[...]
    loop(B - 1, lambda i: sq1_copy(lax.rem(b + 1 + i, B), c).start())
    loop(B, lambda i: sq1_copy(lax.rem(b + i, B), 1 - c).start())

    loop(B - 1, near)
    line(1)

    def sq1_arrived(b_, c_):
        slot = b_ * 2 + c_
        pltpu.make_async_copy(sq1.at[slot], sq1.at[slot], s1_recv.at[slot]).wait()

    loop(B - 1, lambda i: sq1_arrived(lax.rem(b + 1 + i, B), c))
    loop(B, lambda i: sq1_arrived(lax.rem(b + i, B), 1 - c))
    acc = sq1[0]
    for i in range(1, 2 * B):
        acc = acc + sq1[i]
    sq2[a] = acc
    loop(A - 1, lambda i: sq2_copy(lax.rem(a + 1 + i, A)).start())

    for k in range(2, A):
        line(k)
        if k > 2:
            across(k - 2)
            far_y(k - 2)
    for k in range(max(A - 2, 1), A):
        across(k)
        far_y(k)

    def sq2_arrived(i):
        slot = lax.rem(a + 1 + i, A)
        pltpu.make_async_copy(sq2.at[slot], sq2.at[slot], s2_recv.at[slot]).wait()

    loop(A - 1, sq2_arrived)
    acc = sq2[0]
    for i in range(1, A):
        acc = acc + sq2[i]
    eig = acc / (rows * total)
    damped = eig + 0.1 * jnp.mean(eig, axis=1, keepdims=True)
    inv = 1.0 / damped

    def project(l):
        scaled = (rot[l] * inv[l : l + 1, :]).astype(jnp.bfloat16)
        g[:, l * feature : (l + 1) * feature] = lax.dot_general(
            scaled, bv[l], NT, preferred_element_type=jnp.float32
        ).astype(jnp.bfloat16)

    for l in range(0, layers // 2):
        project(l)
    for k in range(1, A):
        rest(k)
    for l in range(layers // 2, layers):
        project(l)
    columns(lambda b_: last(at(a, b_, c, theirs + 1)))
    for k in range(1, A):
        rest_far(k)
    own.wait()

    group = math.gcd(half, 8)
    chunks = half // group

    def score(first):
        cols = []
        for p in range(4):
            for j in range(part):
                cols.append(
                    jnp.concatenate(
                        [qall[(first + i) * 4 + p, j].astype(jnp.float32) for i in range(group)], axis=0
                    ).astype(jnp.bfloat16)
                )
        q = jnp.concatenate(cols, axis=1)
        r = lax.dot_general(q, g[...], NT, preferred_element_type=jnp.float32)
        return r.reshape(group, blk, rows)

    def do_chunk(c_, k):
        r = score(c_ * half + k * group)
        out_ref[pl.ds(k * group, group), pl.ds(c_, 1)] = r.reshape(group, 1, blk, rows)

    loop(chunks, lambda k: do_chunk(c, k))

    def mate(i):
        for p in range(4):
            arrived(((1 - c) * half + i) * 4 + p)

    pl.loop(0, half)(mate)
    loop(chunks, lambda k: do_chunk(1 - c, k))

    def drain(count, sem):
        pltpu.make_async_copy(qall.at[pl.ds(0, count)], qall.at[pl.ds(0, count)], sem).wait()

    drain(2 * (A - 1), z_send)
    drain(3 * A * (B - 1), y_send)
    drain(2 * (A - 1) + A * (B - 1), x_send)
    drain(4 * half, c_send)
    pltpu.make_async_copy(sq1.at[pl.ds(0, 2 * B - 1)], sq1.at[pl.ds(0, 2 * B - 1)], s1_send).wait()
    pltpu.make_async_copy(sq2.at[pl.ds(0, A - 1)], sq2.at[pl.ds(0, A - 1)], s2_send).wait()


def local(n, train_grads, queries, basis):
    rows, layers, feature = train_grads.shape
    blk = queries.shape[0]
    half = n // 2
    A = 2 ** ((half.bit_length()) // 2)
    B = half // A
    t = train_grads.transpose(1, 0, 2)
    q = queries.transpose(1, 0, 2).reshape(4, layers // 4, blk, feature)
    dma = pltpu.SemaphoreType.DMA
    anyspec = pl.BlockSpec(memory_space=pl.ANY)
    out = pl.pallas_call(
        functools.partial(kernel, A, B),
        out_shape=jax.ShapeDtypeStruct((half, 2, blk, rows), jnp.float32),
        in_specs=[anyspec] * 3,
        out_specs=pl.BlockSpec(memory_space=pltpu.VMEM),
        scratch_shapes=[
            pltpu.VMEM((layers, rows, feature), jnp.bfloat16),
            pltpu.VMEM((layers, feature, feature), jnp.bfloat16),
            pltpu.VMEM((layers, rows, feature), jnp.float32),
            pltpu.VMEM((rows, layers * feature), jnp.bfloat16),
            pltpu.VMEM((n * 4, layers // 4, blk, feature), jnp.bfloat16),
            pltpu.VMEM((layers, feature), jnp.float32),
            pltpu.VMEM((2 * B, layers, feature), jnp.float32),
            pltpu.VMEM((A, layers, feature), jnp.float32),
            dma((layers,)),
            dma((layers,)),
            dma,
            dma((n * 4,)),
            dma, dma, dma, dma, dma, dma,
            dma((2 * B,)),
            dma((A,)),
        ],
        compiler_params=pltpu.CompilerParams(
            collective_id=0, has_side_effects=True, vmem_limit_bytes=VMEM_BYTES
        ),
        cost_estimate=pl.CostEstimate(
            flops=4 * layers * rows * feature * feature + 2 * n * blk * rows * layers * feature,
            bytes_accessed=2 * layers * feature * (rows + feature + blk) + 4 * n * blk * rows,
            transcendentals=0,
        ),
    )(t, q, basis)
    return out.reshape(n * blk, rows)


def solution(mesh):
    placed = (P(("slab", "ex"), None, None), P("ex", None, None), P())
    return jax.shard_map(
        functools.partial(local, mesh.shape["ex"]), mesh=mesh, in_specs=placed,
        out_specs=P(None, ("slab", "ex")), check_vma=False,
    )
```

time: 29.5 us -> 27.9 us (0.946)
  Pallas kernels: 27.3 us -> 25.9 us
    pallas_call x1, Pallas kernels: 27.3 us -> 25.9 us  [local(): pl.pallas_call(functools.partial(kernel, A, B), out_shape=jax.ShapeDtypeS...]
    unnamed x1 -> x3, local copies, waits for them, and re-layouts: 2.06 us -> 1.79 us
where the time goes in v2:
time: 27.9 us; the launch traced here: 27.7 us
  Pallas kernels  25.9 us (93%)
  local copies, waits for them, and re-layouts  1.79 us (6%)
    pallas_call x1, Pallas kernels, local(): pl.pallas_call(functools.partial(kernel, A, B), out_shape=jax.ShapeDtypeS...  25.9 us
    unnamed x3, local copies, waits for them, and re-layouts  1.79 us

profile of v2, /device:TPU:0, one launch (start us, length us, event | category | flops | bytes accessed | tf_op | source)
XLA Modules:
  0.0 27.7 jit_solution(10449683995871914093)
XLA Ops:
  0.0 0.0 copy-start
  0.0 0.9 %copy-done = bf16[24,12,256]{2,0,1:T(8,128)(2,1)S(1)} copy-done((bf16[24,12,256]{2,0,1:T(8,128)(2,1)S(1)}, bf16[24,12,256]{2,0,1:T(8,128)(2,1)}, u32[]{:S(2)}) %copy-start) | copy-done | bytes 147480
  0.9 25.9 %shard_map.37 = f32[8,2,24,512]{3,2,1,0:T(8,128)S(1)} custom-call(bf16[12,512,256]{2,1,0:T(8,128)(2,1)} %bitcast.7, bf16[4,3,24,256]{3,2,1,0:T(8,128)(2,1)S(1)} %bitcast.6, bf16[12,256,256]{2,1,0:T(8,128)(2,1)} %b_hbm.1), custom_call_target="tpu_custom_call" | custom-call | flops 2818572288 | bytes 5652480 | tf_op jit(solution)/shard_map/pallas_call | solution.py:310
  26.8 0.9 %copy.5 = f32[384,512]{1,0:T(8,128)} copy(f32[384,512]{1,0:T(8,128)S(1)} %bitcast.5) | data formatting | bytes 1572864
Async XLA Ops:
  0.0 0.9 %copy-start = (bf16[24,12,256]{2,0,1:T(8,128)(2,1)S(1)}, bf16[24,12,256]{2,0,1:T(8,128)(2,1)}, u32[]{:S(2)}) copy-start(bf16[24,12,256]{2,0,1:T(8,128)(2,1)} %param.4) | copy-start | bytes 442372

commit v3 on v2

--- a/solution.py
+++ b/solution.py
@@ -252,39 +252,54 @@
         rest(k)
     for l in range(layers // 2, layers):
         project(l)
-    columns(lambda b_: last(at(a, b_, c, theirs + 1)))
-    for k in range(1, A):
-        rest_far(k)
     own.wait()
 
     group = math.gcd(half, 8)
     chunks = half // group
 
-    def score(first):
+    depth = 2 * part * feature
+
+    def score(first, h):
         cols = []
-        for p in range(4):
+        for t in range(2):
             for j in range(part):
                 cols.append(
                     jnp.concatenate(
-                        [qall[(first + i) * 4 + p, j].astype(jnp.float32) for i in range(group)], axis=0
+                        [qall[(first + i) * 4 + 2 * h + t, j].astype(jnp.float32) for i in range(group)], axis=0
                     ).astype(jnp.bfloat16)
                 )
         q = jnp.concatenate(cols, axis=1)
-        r = lax.dot_general(q, g[...], NT, preferred_element_type=jnp.float32)
-        return r.reshape(group, blk, rows)
-
-    def do_chunk(c_, k):
-        r = score(c_ * half + k * group)
-        out_ref[pl.ds(k * group, group), pl.ds(c_, 1)] = r.reshape(group, 1, blk, rows)
-
-    loop(chunks, lambda k: do_chunk(c, k))
-
-    def mate(i):
-        for p in range(4):
-            arrived(((1 - c) * half + i) * 4 + p)
-
-    pl.loop(0, half)(mate)
-    loop(chunks, lambda k: do_chunk(1 - c, k))
+        gs = g[:, pl.ds(pl.multiple_of(h * depth, depth), depth)]
+        return lax.dot_general(q, gs, NT, preferred_element_type=jnp.float32).reshape(group, 1, blk, rows)
+
+    def do_half(c_, h, add):
+        def one(k):
+            place = (pl.ds(k * group, group), pl.ds(c_, 1))
+            r = score(c_ * half + k * group, h)
+            out_ref[place] = out_ref[place] + r if add else r
+
+        loop(chunks, one)
+
+    def mate(h):
+        def one(i):
+            for t in range(2):
+                arrived(((1 - c) * half + i) * 4 + 2 * h + t)
+
+        pl.loop(0, half)(one)
+
+    do_half(c, s, False)
+    columns(lambda b_: last(at(a, b_, c, theirs + 1)))
+    if True:
+        mate(s)
+        do_half(1 - c, s, False)
+    for k in range(1, A):
+        rest_far(k)
+    do_half(c, 1 - s, True)
+    if not True:
+        mate(s)
+        do_half(1 - c, s, False)
+    mate(1 - s)
+    do_half(1 - c, 1 - s, True)
 
     def drain(count, sem):
         pltpu.make_async_copy(qall.at[pl.ds(0, count)], qall.at[pl.ds(0, count)], sem).wait()

time: 27.9 us -> 26.9 us (0.964)
  Pallas kernels: 25.9 us -> 24.9 us
    pallas_call x1, Pallas kernels: 25.9 us -> 24.9 us  [local(): pl.pallas_call(functools.partial(kernel, A, B), out_shape=jax.ShapeDtypeS...]
where the time goes in v3:
time: 26.9 us; the launch traced here: 26.7 us
  Pallas kernels  24.9 us (93%)
  local copies, waits for them, and re-layouts  1.79 us (7%)
    pallas_call x1, Pallas kernels, local(): pl.pallas_call(functools.partial(kernel, A, B), out_shape=jax.ShapeDtypeS...  24.9 us
    unnamed x3, local copies, waits for them, and re-layouts  1.79 us

profile of v3, /device:TPU:0, one launch (start us, length us, event | category | flops | bytes accessed | tf_op | source)
XLA Modules:
  0.0 26.7 jit_solution(4199541828173854692)
XLA Ops:
  0.0 0.0 copy-start
  0.0 0.9 %copy-done = bf16[24,12,256]{2,0,1:T(8,128)(2,1)S(1)} copy-done((bf16[24,12,256]{2,0,1:T(8,128)(2,1)S(1)}, bf16[24,12,256]{2,0,1:T(8,128)(2,1)}, u32[]{:S(2)}) %copy-start) | copy-done | bytes 147480
  0.9 24.9 %shard_map.37 = f32[8,2,24,512]{3,2,1,0:T(8,128)S(1)} custom-call(bf16[12,512,256]{2,1,0:T(8,128)(2,1)} %bitcast.7, bf16[4,3,24,256]{3,2,1,0:T(8,128)(2,1)S(1)} %bitcast.6, bf16[12,256,256]{2,1,0:T(8,128)(2,1)} %b_hbm.1), custom_call_target="tpu_custom_call" | custom-call | flops 2818572288 | bytes 5652480 | tf_op jit(solution)/shard_map/pallas_call | solution.py:325
  25.8 0.9 %copy.5 = f32[384,512]{1,0:T(8,128)} copy(f32[384,512]{1,0:T(8,128)S(1)} %bitcast.5) | data formatting | bytes 1572864
Async XLA Ops:
  0.0 0.9 %copy-start = (bf16[24,12,256]{2,0,1:T(8,128)(2,1)S(1)}, bf16[24,12,256]{2,0,1:T(8,128)(2,1)}, u32[]{:S(2)}) copy-start(bf16[24,12,256]{2,0,1:T(8,128)(2,1)} %param.4) | copy-start | bytes 442372
